TPU v7x, 256 devices: a whole 4x4x8 slice. The times are simulated.
256 devices in a mesh: dp: 64 (over z, y, core), mp: 4 (over x).
Axes of the slice: x: 4, y: 4, z: 8, core: 2. Of those that a mesh axis runs over, the one named last changes fastest.
Arguments:
- queries: bfloat16 [16384, 4096], P('dp', 'mp'), may hold values from -160 to 160
- passages: bfloat16 [32768, 4096], P('dp', 'mp'), may hold values from -20 to 20
- pos_ids: int32 [512], P('dp'), may hold values from 0 to 1023, as said below
- neg_ids: int32 [512, 7], P('dp'), may hold values from -1 to 1023, as said below
- counts: int32 [512], P('dp'), may hold values from 1 to 7, as said below
Outputs:
- loss_rows: float32 [16384], P('dp')
- query_grad: bfloat16 [16384, 4096], P('dp', 'mp')
- passage_grad: bfloat16 [32768, 4096], P('dp', 'mp')
Inputs may be any that keep to these rules, and one draw needn't show every extreme that they name: `pos_ids`: block g belongs to the index g // 16 of dp. Within the 8 query blocks of one index of dp, the positives and live negatives never name two different blocks of the same index of dp; within one query block they name distinct indices of dp. `neg_ids`: slots at counts and beyond hold -1; live slots name passage blocks. `counts`: some query block has 7 live slots in every draw.
All inputs are finite; a program needn't handle non-finite values.
Results may differ from a plain program's by a relative error of at most 0.011.
Values may be sent and summed in bfloat16 or wider, within the bound.
A program may use at most 128 MiB of HBM per device.

v0:
```python
import jax
import jax.numpy as jnp
from jax import lax
from jax.experimental import pallas as pl
from jax.experimental.pallas import tpu as pltpu
from jax.sharding import PartitionSpec as P

D = 4096
BR = 32
NZ, NY, NC, NX = 8, 4, 2, 4
RY = (0, 1, 3, 2)
W = 1024
QR = 256
PR = 512
MESH = pl.DeviceIdType.MESH
F32 = jnp.float32
BF16 = jnp.bfloat16


def index_of(dy, dc):
    return RY.index(dy % NY) * NC + dc


def dot(a, b, ca, cb):
    return lax.dot_general(a, b, (((ca,), (cb,)), ((), ())), preferred_element_type=F32)


def kernel(pos_hbm, neg_hbm, cnt_hbm, q_hbm, p_hbm, loss_ref, qg_ref, pg_ref,
           qb, pb, psel, bsel, bback, meta, sels, selt, ask, st, srv, lg, stat, norm, wt, lossb,
           gf, gsp, gsm, grp, grm, pn, rb, acc, qrow, wrow, pos_ref, neg_ref, cnt_ref,
           lsem, qs, qr, ps, pr, sibs, sibr, ms, mr, es, er, ss, sr, ts, tr, ws, wr, ls, lr, gs, gr, ns, nr, ys, yr, fs, fr, vs, vr):
    dp = lax.axis_index("dp")
    x = lax.axis_index("mp")
    z = dp // (NY * NC)
    y = lax.rem(dp // NC, NY)
    c = lax.rem(dp, NC)
    xm, xh = lax.rem(x, 2), x // 2

    def dev(dz=0, dy=0, dc=0, dx=0):
        there = lax.rem(z + dz, NZ) * (NY * NC) + lax.rem(y + dy, NY) * NC + lax.rem(c + dc, NC)
        return (there, lax.rem(x + dx, NX))

    row = [(RY[o // NC], o % NC) for o in range(8)]
    peers = [dev(dz=d) for d in range(1, NZ)] + [dev(dy=a, dc=b) for a, b in row[1:]] + [dev(dx=d) for d in range(1, NX)]
    barrier = pltpu.get_barrier_semaphore()
    for p in peers:
        pl.semaphore_signal(barrier, 1, device_id=p, device_id_type=MESH)

    lists = [pltpu.make_async_copy(a, b, lsem.at[2 + n]) for n, (a, b) in enumerate(((pos_hbm, pos_ref), (neg_hbm, neg_ref), (cnt_hbm, cnt_ref)))]
    for one in lists:
        one.start()
    load_q = pltpu.make_async_copy(q_hbm, qb.at[0], lsem.at[0])
    load_p = pltpu.make_async_copy(p_hbm, pb.at[0, 0], lsem.at[1])
    load_q.start()
    load_p.start()

    sent = []

    def remote(src, dst, ssem, rsem, to):
        return pltpu.make_async_remote_copy(src_ref=src, dst_ref=dst, send_sem=ssem, recv_sem=rsem, device_id=to, device_id_type=MESH)

    def send(*args, when=None):
        if when is None:
            remote(*args).start()
        else:
            @pl.when(when)
            def _():
                remote(*args).start()
        sent.append((args, when))

    def arrived(dst, rsem):
        remote(dst, dst, rsem, rsem, peers[0]).wait_recv()

    def rows(i, n=64):
        return pl.ds(i * n, n)

    def send_q(k, j):
        i = k * 4 + j
        right, left = (q_hbm, q_hbm) if k == 0 else (qb.at[8 - k], qb.at[k])
        send(right.at[rows(j)], qb.at[7 - k, rows(j)], qs.at[0, i], qr.at[0, i], dev(dz=1))
        jm = (j + 2) % 4
        send(left.at[rows(jm)], qb.at[k + 1, rows(jm)], qs.at[1, i], qr.at[1, i], dev(dz=NZ - 1))

    def q_arrived(k, j):
        i = (k - 1) * 4 + j
        arrived(qb.at[8 - k, rows(j)], qr.at[0, i])
        arrived(qb.at[k, rows((j + 2) % 4)], qr.at[1, i])

    def send_row_q(t):
        up, down = (qb.at[0], qb.at[0]) if t < 4 else (qrow.at[3, 0], qrow.at[1, 0])
        a, b = (3, 1) if t < 4 else (2, 2)
        ip, im = (t, (t + 2) % 4) if t < 4 else (t - 4, t - 2)
        send(up.at[rows(ip)], qrow.at[a, 0, rows(ip)], ys.at[0, t], yr.at[0, t], dev(dy=1))
        send(down.at[rows(im)], qrow.at[b, 0, rows(im)], ys.at[1, t], yr.at[1, t], dev(dy=NY - 1))

    def row_q_arrived(t):
        a, b = (3, 1) if t < 4 else (2, 2)
        ip, im = (t, (t + 2) % 4) if t < 4 else (t - 4, t - 2)
        arrived(qrow.at[a, 0, rows(ip)], yr.at[0, t])
        arrived(qrow.at[b, 0, rows(im)], yr.at[1, t])

    def send_row_sib(a):
        send(qb.at[0] if a == 0 else qrow.at[a, 0], qrow.at[a, 1], fs.at[a], fr.at[a], dev(dc=1))

    def p_part(t):
        if t < 8:
            return t, (t + 4) % 8
        return t - 8, t - 4

    def send_p(t):
        ip, im = p_part(t)
        up, down = (p_hbm, p_hbm) if t < 8 else (pb.at[3, 0], pb.at[1, 0])
        a, b = (3, 1) if t < 8 else (2, 2)
        send(up.at[rows(ip)], pb.at[a, 0, rows(ip)], ps.at[0, t], pr.at[0, t], dev(dy=1))
        send(down.at[rows(im)], pb.at[b, 0, rows(im)], ps.at[1, t], pr.at[1, t], dev(dy=NY - 1))

    def send_sib(a, i, n, k):
        send((p_hbm if a == 0 else pb.at[a, 0]).at[rows(i, n)], pb.at[a, 1, rows(i, n)], sibs.at[k], sibr.at[k], dev(dc=1))

    def sib_arrived(a):
        if a == 2:
            for i in range(8):
                arrived(pb.at[2, 1, rows(i)], sibr.at[8 + i])
        else:
            for half in range(2):
                arrived(pb.at[a, 1, rows(half, 256)], sibr.at[2 * a + half])

    for one in lists:
        one.wait()
    lane = lax.broadcasted_iota(jnp.int32, (8, 128), 1)
    sub8 = lax.broadcasted_iota(jnp.int32, (8, 128), 0)
    o_l = lane & 7
    og = o_l >> 1
    ry_l = og ^ (og >> 1)
    owner = (((z + (lane >> 3)) & 7) << 3) + (((y + ry_l) & 3) << 1) + (c ^ (o_l & 1))
    owner = jnp.where(lane < 64, owner, -7)
    code = jnp.zeros((8, 128), jnp.int32)
    sel = jnp.full((8, 128), -1, jnp.int32)
    for s in range(8):
        col = jnp.full((8, 128), -1, jnp.int32)
        for b in range(8):
            block = pos_ref[b] if s == 0 else jnp.where(s - 1 < cnt_ref[b], neg_ref[b, s - 1], -1)
            col = jnp.where(sub8 == b, block, col)
        hit = (col >= 0) & ((col >> 4) == owner)
        code = jnp.where(hit, 2 if s == 0 else 1, code)
        sel = jnp.where(hit, col & 15, sel)
    sel = jnp.broadcast_to(jnp.max(sel, axis=0, keepdims=True), (8, 128))
    meta[0] = jnp.concatenate([code, sel], axis=0).astype(F32).astype(BF16)
    pl.semaphore_wait(barrier, len(peers))
    for d in range(1, NZ):
        send(meta.at[0], meta.at[8 - d], ms.at[d - 1], mr.at[7 - d], dev(dz=d))
    for j in range(4):
        send_q(0, j)
        send_p(j)
    for t in range(4, 8):
        send_p(t)
    send_sib(0, 0, 256, 0)
    send_sib(0, 1, 256, 1)

    def my_home(p):
        return lax.rem(p + 4 * xm - z + 8, 8)

    def take_lists():
        for r in range(1, NZ):
            arrived(meta.at[r], mr.at[r - 1])
        sub16 = lax.broadcasted_iota(jnp.int32, (16, 128), 0)
        table = jnp.zeros((16, 128), F32)
        for r in range(NZ):
            own = meta[r].astype(F32)[8:16]
            pair = jnp.concatenate([own, own], axis=0)
            table = jnp.where(sub16 == r, pair, table)
            for k in range(4):
                selt[r, pl.ds(8 * k, 8), :] = own * 32.0 + (sub8 + 8 * k).astype(F32)
        sels[0] = table.astype(BF16)
        for o in range(1, 8):
            dy, dc = row[o]
            back = index_of(-dy, dc)
            send(sels.at[0], sels.at[back], es.at[o - 1], er.at[back - 1], dev(dy=dy, dc=dc))
        for p in range(4):
            r = my_home(p)
            t = lax.rem(8 - r, 8)
            down = (lax.broadcasted_iota(jnp.int32, (QR, 128), 1)
                    == t * 8 + (lax.broadcasted_iota(jnp.int32, (QR, 128), 0) >> 5)).astype(F32).astype(BF16)
            across = (lax.broadcasted_iota(jnp.int32, (16, 128), 0)
                      == xh * 4 + (lax.broadcasted_iota(jnp.int32, (16, 128), 1) >> 5)).astype(F32).astype(BF16)
            ask[p] = dot(dot(down, meta[r], 1, 1).astype(BF16), across, 1, 0)

    jl = lax.broadcasted_iota(jnp.int32, (BR, PR), 1).astype(F32)

    def pick(o):
        dy, dc = row[o]
        for r in range(NZ):
            k = ((8 - r) % 8) * 8 + o
            want = jnp.broadcast_to(selt[r, :, k:k + 1], (BR, PR))
            bsel[pl.ds(r * BR, BR), :] = (want == jl).astype(F32).astype(BF16)

        def part(n, _):
            cols = pl.ds(pl.multiple_of(n * 256, 256), 256)
            got = dot(bsel[...], pb[dy, dc, :, cols], 1, 0).astype(BF16)
            for r in range(NZ):
                psel[r, pl.ds(o * BR, BR), cols] = got[r * BR:(r + 1) * BR]
            return 0

        lax.fori_loop(0, 4, part, 0)

    bounds = (0, 64, 192, 256)

    def score(r, gs_, halves):
        home = lax.rem(z + r, 8)
        p, m = lax.rem(home, 4), home // 4
        part = pl.ds(bounds[gs_[0]], bounds[gs_[-1] + 1] - bounds[gs_[0]])
        first, n = halves[0] * 128, len(halves) * 128
        got = dot(psel[r, part, :], qb[r, pl.ds(first, n), :], 1, 1)
        for half in halves:
            xt = m + 2 * half
            st[p, xt, part, :] = got[:, half * 128 - first:half * 128 - first + 128]
            slot = lax.rem(x - xt + 4, 4) - 1
            send(st.at[p, xt, part], srv.at[p, slot, part], ss.at[r, gs_[0], half], sr.at[p, slot], (dp, xt), when=xt != x)

    rowi = lax.broadcasted_iota(jnp.int32, (QR, 128), 0)
    lanei = lax.broadcasted_iota(jnp.int32, (QR, 128), 1)
    same_row = (rowi & 31) == (lanei & 31)

    def send_stats(n):
        for d in range(1, NZ):
            send(stat.at[n, 0], stat.at[n, 8 - d], ts.at[n, d - 1], tr.at[n, 7 - d], dev(dz=d))

    def row_stats():
        scale = jnp.zeros((8, 128), F32)
        hits = jnp.zeros((8, 128), F32)
        for n in (2, 1, 3, 0):
            p = lax.rem(z + n, 4)
            for k in range(3):
                arrived(srv.at[p, k], sr.at[p, k])
            summed = st[p, x] + srv[p, 0] + srv[p, 1] + srv[p, 2]
            live = ask[p] > 0.5
            logits = jnp.where(live, summed * (D ** -0.5), -1e30)
            lg[p] = logits
            top = jnp.max(logits, axis=0, keepdims=True)
            total = jnp.sum(jnp.where(live, jnp.exp(logits - top), 0.0), axis=0, keepdims=True)
            pos = jnp.sum(jnp.where((ask[p] > 1.5) & same_row, logits, 0.0), axis=0, keepdims=True)
            scale = jnp.where(sub8 == p, top, jnp.where(sub8 == 4 + p, total, scale))
            hits = jnp.where(sub8 == p, pos, hits)
        stat[0, 0] = scale
        stat[1, 0] = hits
        send_stats(0)

    def prepare(r):
        line = lax.broadcasted_iota(jnp.int32, (1, QR), 1)
        want = jnp.zeros((1, QR), F32)
        for j in range(8):
            dy, dc = row[j]
            k = ((8 - r) % 8) * 8 + index_of(-dy, dc)
            asked = jnp.broadcast_to(sels[j].astype(F32)[r:r + 1, k:k + 1], (1, QR))
            want = jnp.where((line >> 5) == j, asked * 32.0 + (line & 31).astype(F32), want)
        down = lax.broadcasted_iota(jnp.int32, (PR, QR), 0).astype(F32)
        bback[r] = (down == want).astype(F32).astype(BF16)

    here, scored = {(0, 0), (0, 1)}, set()

    def slot_events(t):
        k, j = t // 4 + 1, t % 4
        q_arrived(k, j)
        if k < 3 or (k == 3 and j < 2):
            send_q(k, j)
        if k == 4 and j == 1:
            here.update(((4, 0), (4, 1)))
        elif k < 4 and j % 2:
            here.update(((8 - k, j // 2), (k, 1 - j // 2)))
        if t < 12:
            ip, im = p_part(t)
            a, b = (3, 1) if t < 8 else (2, 2)
            arrived(pb.at[a, 0, rows(ip)], pr.at[0, t])
            arrived(pb.at[b, 0, rows(im)], pr.at[1, t])
            if t < 4:
                send_p(t + 8)
            if t == 3:
                send_sib(3, 0, 256, 6)
                send_sib(1, 1, 256, 3)
            if t == 7:
                send_sib(3, 1, 256, 7)
                send_sib(1, 0, 256, 2)
            if t > 7:
                send_sib(2, ip, 64, 8 + ip)
                send_sib(2, im, 64, 8 + im)

    def score_new(upto):
        for r in (1, 5, 2, 6, 3, 7, 0, 4):
            todo = {}
            for half in range(2):
                left = tuple(g for g in range(upto + 1) if (r, half) in here and (r, g, half) not in scored)
                if left:
                    todo.setdefault(left, []).append(half)
            for left, halves in todo.items():
                score(r, left, halves)
                scored.update((r, g, half) for g in left for half in halves)

    for t in range(14):
        slot_events(t)
        if t == 0:
            take_lists()
            load_q.wait()
            load_p.wait()
        if t == 1:
            pick(0)
        if t == 2:
            sib_arrived(0)
            pick(1)
        if t == 9:
            for o in range(1, 8):
                arrived(sels.at[o], er.at[o - 1])
        if 9 <= t < 11:
            prepare(2 * t - 18)
            prepare(2 * t - 17)
        if t == 7:
            pick(2)
            pick(4)
            sib_arrived(1)
            pick(3)
            sib_arrived(3)
            pick(5)
        if 2 <= t < 7:
            score_new(0)
        if 7 <= t < 12:
            score_new(1)
        if t == 11:
            pick(6)
            sib_arrived(2)
            pick(7)
            for n in range(4):
                send_row_q(n)
            send_row_sib(0)
        if t >= 11:
            score_new(2)
    for n in range(2):
        row_q_arrived(n)
        send_row_q(n + 4)
    assert len(scored) == 48
    row_stats()
    for r in range(4, 8):
        prepare(r)
    row_q_arrived(2)
    row_q_arrived(3)
    send_row_sib(1)
    send_row_sib(3)

    for d in range(1, NZ):
        arrived(stat.at[0, d], tr.at[0, d - 1])
    top = stat[0, 0, 0:4]
    for d in range(1, NZ):
        top = jnp.maximum(top, stat[0, d, 0:4])
    total = jnp.zeros((4, 128), F32)
    for d in range(NZ):
        total = total + stat[0, d, 4:8] * jnp.exp(stat[0, d, 0:4] - top)
    norm[0:4] = top
    norm[4:8] = 1.0 / total

    def weigh(s):
        p = lax.rem(z + s, 4)
        r = my_home(p)
        hot = jnp.where((ask[p] > 1.5) & same_row, 1.0, 0.0)
        wt[r, xh] = (jnp.exp(lg[p] - norm[pl.ds(p, 1), :]) * norm[pl.ds(4 + p, 1), :] - hot).astype(BF16)
        for d in range(1, NX):
            send(wt.at[r, xh], wt.at[r, xh], ws.at[s, d - 1], wr.at[r, xh], dev(dx=d))

    weigh(0)
    weigh(3)
    def weights_arrived(r):
        home = lax.rem(z + r, 8)
        for half in range(2):
            @pl.when(home // 4 + 2 * half != x)
            def _():
                arrived(wt.at[r, half], wr.at[r, half])

    def weights(r):
        return jnp.concatenate([wt[r, 0], wt[r, 1]], axis=1)

    def panels(r):
        def part(n, _):
            cols = pl.ds(pl.multiple_of(n * 256, 256), 256)
            pn[r, :, cols] = dot(weights(r), qb[r, :, cols], 1, 0).astype(BF16)
            return 0

        lax.fori_loop(0, 4, part, 0)
        for o in range(1, 8):
            dy, dc = row[o]
            back = index_of(-dy, dc)
            send(pn.at[r, pl.ds(o * BR, BR)], rb.at[r, pl.ds(back * BR, BR)], ns.at[r, o - 1], nr.at[r, back - 1],
                 dev(dy=dy, dc=dc))
        rb[r, pl.ds(0, BR), :] = pn[r, pl.ds(0, BR), :]

    def grads(r):
        def part(n, _):
            cols = pl.ds(pl.multiple_of(n * 256, 256), 256)
            gf[r, :, cols] = dot(weights(r), psel[r, :, cols], 0, 0)
            return 0

        lax.fori_loop(0, 4, part, 0)

    def pass_on(side, h, i, add):
        mineb, came = (gsp, grp) if side == 0 else (gsm, grm)
        r = 4 - h if side == 0 else (4 + h) % 8
        value = gf[r, rows(i), :]
        if add:
            arrived(came.at[h - 1, rows(i)], gr.at[side, h - 1, i])
            value = value + came[h - 1, rows(i), :].astype(F32)
        mineb[h, rows(i), :] = value.astype(BF16)
        send(mineb.at[h, rows(i)], came.at[h, rows(i)], gs.at[side, h, i], gr.at[side, h, i],
             dev(dz=1 if side == 0 else NZ - 1))

    weights_arrived(4)
    weigh(1)
    panels(4)
    grads(4)
    for k in range(2):
        pass_on(0, 0, k, False)
        pass_on(1, 0, 2 + k, False)
    send_stats(1)
    weights_arrived(3)
    weigh(2)
    row_q_arrived(4)
    row_q_arrived(5)
    send_row_sib(2)
    weights_arrived(0)
    for o in range(1, 8):
        dy, dc = row[o]
        back = index_of(-dy, dc)
        for half in range(2):
            send(wt.at[0, half, pl.ds(o * BR, BR)], wrow.at[back, half], vs.at[o - 1, half], vr.at[back - 1, half], dev(dy=dy, dc=dc))
    for r in (3, 5):
        if r == 5:
            weights_arrived(r)
        panels(r)
        grads(r)
        for k in range(2):
            pass_on(0 if r == 3 else 1, 1, (2 + k) if r == 3 else k, False)
        weights_arrived((r + 4) % 8)
        panels((r + 4) % 8)
    for k in range(2):
        pass_on(0, 1, k, True)
        pass_on(1, 1, 2 + k, True)
    for r in (2, 6):
        weights_arrived(r)
        grads(r)
        panels(r)
    for h in range(2, 4):
        if h == 3:
            grads(1)
            grads(7)
        for k in range(4):
            pass_on(0, h, (k + 2) % 4, True)
            pass_on(1, h, k, True)
    grads(0)
    for d in range(1, NZ):
        arrived(stat.at[1, d], tr.at[1, d - 1])
    pos = jnp.zeros((4, 128), F32)
    for d in range(NZ):
        pos = pos + stat[1, d, 0:4]
    losses = (top - pos) + jnp.log(total)
    own_pair = lax.rem(z, 4)
    tile = jnp.zeros((1, 128), F32)
    for p in range(4):
        tile = jnp.where(own_pair == p, losses[p:p + 1], tile)
    lossb[x] = jnp.broadcast_to(tile, (8, 128))
    for d in range(1, NX):
        send(lossb.at[x], lossb.at[x], ls.at[d - 1], lr.at[3 - d], dev(dx=d))

    def row_panels():
        for a in range(NY):
            arrived(qrow.at[a, 1], fr.at[a])
        for j in range(8):
            dy, dc = row[j]
            if j:
                for half in range(2):
                    arrived(wrow.at[j, half], vr.at[j - 1, half])
            w = [wrow[j, half] if j else wt[0, half, 0:BR, :] for half in range(2)]
            w = jnp.concatenate(w, axis=1)
            q = qrow.at[dy, dc] if j else qb.at[0]
            rb[0, pl.ds(j * BR, BR), :] = dot(w, q[...], 1, 0).astype(BF16)

    def collect(r, first=False, last=False):
        if r:
            for j in range(1, 8):
                arrived(rb.at[r, pl.ds(j * BR, BR)], nr.at[r, j - 1])
        else:
            row_panels()

        for n in range(4):
            cols = pl.ds(n * 256, 256)
            term = dot(bback[r], rb[r, :, cols], 1, 0)
            term = term if first else acc[:, cols] + term
            if last:
                pg_ref[:, cols] = term.astype(BF16)
            else:
                acc[:, cols] = term

    for n, r in enumerate((4, 0, 3, 7, 5, 1, 2)):
        collect(r, first=n == 0)
    for k in range(4):
        ip, im = (k + 2) % 4, k
        arrived(grp.at[3, rows(ip)], gr.at[0, 3, ip])
        arrived(grm.at[3, rows(im)], gr.at[1, 3, im])
    for k in range(4):
        qg_ref[rows(k), :] = (gf[0, rows(k), :] + grp[3, rows(k), :].astype(F32) + grm[3, rows(k), :].astype(F32)).astype(BF16)
    for d in range(1, NX):
        other = lax.rem(x + d, NX)
        arrived(lossb.at[other], lr.at[d - 1])
    for half in range(2):
        loss_ref[half:half + 1, :] = lossb[z // 4 + 2 * half][0:1]
    for args, when in sent:
        if when is None:
            remote(*args).wait_send()
        else:
            @pl.when(when)
            def _():
                remote(*args).wait_send()
    collect(6, last=True)


def body(queries, passages, pos_ids, neg_ids, counts):
    dma = pltpu.SemaphoreType.DMA
    vm = pltpu.VMEM
    loss, query_grad, passage_grad = pl.pallas_call(
        kernel,
        out_shape=(pltpu.VMEM((2, 128), F32), pltpu.VMEM((QR, W), BF16), pltpu.VMEM((PR, W), BF16)),
        in_specs=[pl.BlockSpec(memory_space=pl.ANY)] * 5,
        out_specs=tuple([pl.BlockSpec(memory_space=pltpu.VMEM)] * 3),
        scratch_shapes=[
            vm((8, QR, W), BF16), vm((NY, NC, PR, W), BF16), vm((8, QR, W), BF16), vm((QR, PR), BF16), vm((8, PR, QR), BF16),
            vm((8, 16, 128), BF16), vm((8, 16, 128), BF16), vm((8, BR, 128), F32), vm((4, QR, 128), F32),
            vm((4, 4, QR, 128), F32), vm((4, 3, QR, 128), F32), vm((4, QR, 128), F32),
            vm((2, 8, 8, 128), F32), vm((8, 128), F32), vm((8, 2, QR, 128), BF16), vm((NX, 8, 128), F32),
            vm((8, QR, W), F32), vm((4, QR, W), BF16), vm((4, QR, W), BF16), vm((4, QR, W), BF16), vm((4, QR, W), BF16),
            vm((8, QR, W), BF16), vm((8, QR, W), BF16), vm((PR, W), F32),
            vm((NY, NC, QR, W), BF16), vm((8, 2, BR, 128), BF16),
            pltpu.SMEM((8,), jnp.int32), pltpu.SMEM((8, 7), jnp.int32), pltpu.SMEM((8,), jnp.int32),
            dma((5,)), dma((2, 14)), dma((2, 14)), dma((2, 12)), dma((2, 12)), dma((16,)), dma((16,)), dma((7,)), dma((7,)),
            dma((7,)), dma((7,)), dma((8, 3, 2)), dma((4, 3)), dma((2, 7)), dma((2, 7)), dma((4, 3)), dma((8, 2)),
            dma((3,)), dma((3,)), dma((2, 4, 4)), dma((2, 4, 4)), dma((8, 7)), dma((8, 7)), dma((2, 6)), dma((2, 6)), dma((4,)), dma((4,)),
            dma((7, 2)), dma((7, 2)),
        ],
        compiler_params=pltpu.CompilerParams(collective_id=0, has_side_effects=True, vmem_limit_bytes=60 * 2**20),
        cost_estimate=pl.CostEstimate(flops=10**10, bytes_accessed=4 * 10**6, transcendentals=10**6),
    )(pos_ids, neg_ids, counts, queries, passages)
    return loss.reshape(QR), query_grad, passage_grad


def solution(mesh):
    assert mesh.shape["dp"] == NZ * NY * NC and mesh.shape["mp"] == NX
    return jax.shard_map(
        body,
        mesh=mesh,
        in_specs=(P("dp", "mp"), P("dp", "mp"), P("dp"), P("dp", None), P("dp")),
        out_specs=(P("dp"), P("dp", "mp"), P("dp", "mp")),
        check_vma=False,
    )
```

profile of v0, /device:TPU:1, one launch (start us, length us, event | category | flops | bytes accessed | tf_op | source)
XLA Modules:
  0.0 125.6 jit_solution(5388446688672504598)
XLA Ops:
  0.6 122.6 %shard_map.76 = (f32[2,128]{1,0:T(2,128)S(1)}, bf16[256,1024]{1,0:T(8,128)(2,1)S(1)}, bf16[512,1024]{1,0:T(8,128)(2,1)S(1)}) custom-call(s32[8]{0:T(128)} %pos_hbm.1, s32[8,7]{1,0:T(8,128)} %neg_hbm.1, s32[8]{0:T(128)} %cnt_hbm.1, bf16[256,1024]{1,0:T(8,128)(2,1)} %q_hbm.1, bf16[512,1024]{1,0:T(8,128)(2,1)} %p_hbm.1), custom_call_target="tpu_custom_call" | custom-call | flops 10000000000 | bytes 4000000 | tf_op jit(solution)/shard_map/pallas_call | solution.py:523
  123.3 0.6 copy.11
  123.8 0.8 copy.12
  124.6 1.0 copy.13
where the time goes:
time: 126 us
  Pallas kernels  123 us (98%)
  local copies, waits for them, and re-layouts  2.33 us (2%)
    pallas_call x1, Pallas kernels, body(): pl.pallas_call(kernel, out_shape=(pltpu.VMEM((2, 128), F32), pltpu.VMEM((...  123 us

commit v1 on v0

--- a/solution.py
+++ b/solution.py
@@ -187,16 +187,18 @@
 
     jl = lax.broadcasted_iota(jnp.int32, (BR, PR), 1).astype(F32)
 
-    def pick(o):
-        dy, dc = row[o]
+    def choose(o):
         for r in range(NZ):
             k = ((8 - r) % 8) * 8 + o
             want = jnp.broadcast_to(selt[r, :, k:k + 1], (BR, PR))
-            bsel[pl.ds(r * BR, BR), :] = (want == jl).astype(F32).astype(BF16)
+            bsel[o, pl.ds(r * BR, BR), :] = (want == jl).astype(F32).astype(BF16)
+
+    def pick(o):
+        dy, dc = row[o]
 
         def part(n, _):
             cols = pl.ds(pl.multiple_of(n * 256, 256), 256)
-            got = dot(bsel[...], pb[dy, dc, :, cols], 1, 0).astype(BF16)
+            got = dot(bsel[o], pb[dy, dc, :, cols], 1, 0).astype(BF16)
             for r in range(NZ):
                 psel[r, pl.ds(o * BR, BR), cols] = got[r * BR:(r + 1) * BR]
             return 0
@@ -302,7 +304,13 @@
             load_q.wait()
             load_p.wait()
         if t == 1:
+            choose(0)
+            choose(1)
             pick(0)
+        if 3 <= t < 7:
+            choose(t - 1)
+        if 8 <= t < 10:
+            choose(t - 2)
         if t == 2:
             sib_arrived(0)
             pick(1)
@@ -526,7 +534,7 @@
         in_specs=[pl.BlockSpec(memory_space=pl.ANY)] * 5,
         out_specs=tuple([pl.BlockSpec(memory_space=pltpu.VMEM)] * 3),
         scratch_shapes=[
-            vm((8, QR, W), BF16), vm((NY, NC, PR, W), BF16), vm((8, QR, W), BF16), vm((QR, PR), BF16), vm((8, PR, QR), BF16),
+            vm((8, QR, W), BF16), vm((NY, NC, PR, W), BF16), vm((8, QR, W), BF16), vm((8, QR, PR), BF16), vm((8, PR, QR), BF16),
             vm((8, 16, 128), BF16), vm((8, 16, 128), BF16), vm((8, BR, 128), F32), vm((4, QR, 128), F32),
             vm((4, 4, QR, 128), F32), vm((4, 3, QR, 128), F32), vm((4, QR, 128), F32),
             vm((2, 8, 8, 128), F32), vm((8, 128), F32), vm((8, 2, QR, 128), BF16), vm((NX, 8, 128), F32),

time: 126 us -> 125 us (level)
  no operation moved by 1% of the time
where the time goes in v1:
time: 125 us
  Pallas kernels  122 us (98%)
  local copies, waits for them, and re-layouts  2.33 us (2%)
    pallas_call x1, Pallas kernels, body(): pl.pallas_call(kernel, out_shape=(pltpu.VMEM((2, 128), F32), pltpu.VMEM((...  122 us

profile of v1, /device:TPU:1, one launch (start us, length us, event | category | flops | bytes accessed | tf_op | source)
XLA Modules:
  0.0 125.3 jit_solution(11075708079426875287)
XLA Ops:
  0.6 122.3 %shard_map.76 = (f32[2,128]{1,0:T(2,128)S(1)}, bf16[256,1024]{1,0:T(8,128)(2,1)S(1)}, bf16[512,1024]{1,0:T(8,128)(2,1)S(1)}) custom-call(s32[8]{0:T(128)} %pos_hbm.1, s32[8,7]{1,0:T(8,128)} %neg_hbm.1, s32[8]{0:T(128)} %cnt_hbm.1, bf16[256,1024]{1,0:T(8,128)(2,1)} %q_hbm.1, bf16[512,1024]{1,0:T(8,128)(2,1)} %p_hbm.1), custom_call_target="tpu_custom_call" | custom-call | flops 10000000000 | bytes 4000000 | tf_op jit(solution)/shard_map/pallas_call | solution.py:531
  122.9 0.6 copy.11
  123.5 0.8 copy.12
  124.3 1.0 copy.13

commit v2 on v1

--- a/solution.py
+++ b/solution.py
@@ -11,6 +11,7 @@
 RY = (0, 1, 3, 2)
 W = 1024
 QR = 256
+FW = 384
 PR = 512
 MESH = pl.DeviceIdType.MESH
 F32 = jnp.float32
@@ -27,8 +28,8 @@
 
 def kernel(pos_hbm, neg_hbm, cnt_hbm, q_hbm, p_hbm, loss_ref, qg_ref, pg_ref,
            qb, pb, psel, bsel, bback, meta, sels, selt, ask, st, srv, lg, stat, norm, wt, lossb,
-           gf, gsp, gsm, grp, grm, pn, rb, acc, qrow, wrow, pos_ref, neg_ref, cnt_ref,
-           lsem, qs, qr, ps, pr, sibs, sibr, ms, mr, es, er, ss, sr, ts, tr, ws, wr, ls, lr, gs, gr, ns, nr, ys, yr, fs, fr, vs, vr):
+           gf, gsp, gsm, grp, grm, pn, rb, acc, qrow, wrow, qrow2, wrow2, pos_ref, neg_ref, cnt_ref,
+           lsem, qs, qr, ps, pr, sibs, sibr, ms, mr, es, er, ss, sr, ts, tr, ws, wr, ls, lr, gs, gr, ns, nr, ys, yr, fs, fr, vs, vr, ys2, yr2, fs2, fr2, vs2, vr2):
     dp = lax.axis_index("dp")
     x = lax.axis_index("mp")
     z = dp // (NY * NC)
@@ -101,6 +102,22 @@
 
     def send_row_sib(a):
         send(qb.at[0] if a == 0 else qrow.at[a, 0], qrow.at[a, 1], fs.at[a], fr.at[a], dev(dc=1))
+
+    def send_row_q2(t):
+        up, down = (qb.at[7, :, pl.ds(0, FW)], qb.at[7, :, pl.ds(0, FW)]) if t < 4 else (qrow2.at[3, 0], qrow2.at[1, 0])
+        a, b = (3, 1) if t < 4 else (2, 2)
+        ip, im = (t, (t + 2) % 4) if t < 4 else (t - 4, t - 2)
+        send(up.at[rows(ip)], qrow2.at[a, 0, rows(ip)], ys2.at[0, t], yr2.at[0, t], dev(dy=1))
+        send(down.at[rows(im)], qrow2.at[b, 0, rows(im)], ys2.at[1, t], yr2.at[1, t], dev(dy=NY - 1))
+
+    def row_q2_arrived(t):
+        a, b = (3, 1) if t < 4 else (2, 2)
+        ip, im = (t, (t + 2) % 4) if t < 4 else (t - 4, t - 2)
+        arrived(qrow2.at[a, 0, rows(ip)], yr2.at[0, t])
+        arrived(qrow2.at[b, 0, rows(im)], yr2.at[1, t])
+
+    def send_row_sib2(a):
+        send(qb.at[7, :, pl.ds(0, FW)] if a == 0 else qrow2.at[a, 0], qrow2.at[a, 1], fs2.at[a], fr2.at[a], dev(dc=1))
 
     def p_part(t):
         if t < 8:
@@ -343,6 +360,9 @@
     for n in range(2):
         row_q_arrived(n)
         send_row_q(n + 4)
+    for n in range(4):
+        send_row_q2(n)
+    send_row_sib2(0)
     assert len(scored) == 48
     row_stats()
     for r in range(4, 8):
@@ -373,6 +393,9 @@
 
     weigh(0)
     weigh(3)
+    for n in range(2):
+        row_q2_arrived(n)
+        send_row_q2(n + 4)
     def weights_arrived(r):
         home = lax.rem(z + r, 8)
         for half in range(2):
@@ -393,8 +416,12 @@
         for o in range(1, 8):
             dy, dc = row[o]
             back = index_of(-dy, dc)
-            send(pn.at[r, pl.ds(o * BR, BR)], rb.at[r, pl.ds(back * BR, BR)], ns.at[r, o - 1], nr.at[r, back - 1],
+            cols = pl.ds(FW, W - FW) if r == 7 else pl.ds(0, W)
+            send(pn.at[r, pl.ds(o * BR, BR), cols], rb.at[r, pl.ds(back * BR, BR), cols], ns.at[r, o - 1], nr.at[r, back - 1],
                  dev(dy=dy, dc=dc))
+            for half in range(2 if r == 7 else 0):
+                send(wt.at[7, half, pl.ds(o * BR, BR)], wrow2.at[back, half], vs2.at[o - 1, half], vr2.at[back - 1, half],
+                     dev(dy=dy, dc=dc))
         rb[r, pl.ds(0, BR), :] = pn[r, pl.ds(0, BR), :]
 
     def grads(r):
@@ -429,6 +456,10 @@
     row_q_arrived(4)
     row_q_arrived(5)
     send_row_sib(2)
+    row_q2_arrived(2)
+    row_q2_arrived(3)
+    send_row_sib2(1)
+    send_row_sib2(3)
     weights_arrived(0)
     for o in range(1, 8):
         dy, dc = row[o]
@@ -451,6 +482,9 @@
         weights_arrived(r)
         grads(r)
         panels(r)
+    row_q2_arrived(4)
+    row_q2_arrived(5)
+    send_row_sib2(2)
     for h in range(2, 4):
         if h == 3:
             grads(1)
@@ -486,10 +520,23 @@
             q = qrow.at[dy, dc] if j else qb.at[0]
             rb[0, pl.ds(j * BR, BR), :] = dot(w, q[...], 1, 0).astype(BF16)
 
+    def row_panels2():
+        for a in range(NY):
+            arrived(qrow2.at[a, 1], fr2.at[a])
+        for j in range(1, 8):
+            dy, dc = row[j]
+            for half in range(2):
+                arrived(wrow2.at[j, half], vr2.at[j - 1, half])
+            w = jnp.concatenate([wrow2[j, 0], wrow2[j, 1]], axis=1)
+            rb[7, pl.ds(j * BR, BR), pl.ds(0, FW)] = dot(w, qrow2[dy, dc], 1, 0).astype(BF16)
+
     def collect(r, first=False, last=False):
         if r:
+            cols = pl.ds(FW, W - FW) if r == 7 else pl.ds(0, W)
             for j in range(1, 8):
-                arrived(rb.at[r, pl.ds(j * BR, BR)], nr.at[r, j - 1])
+                arrived(rb.at[r, pl.ds(j * BR, BR), cols], nr.at[r, j - 1])
+            if r == 7:
+                row_panels2()
         else:
             row_panels()
 
@@ -540,12 +587,12 @@
             vm((2, 8, 8, 128), F32), vm((8, 128), F32), vm((8, 2, QR, 128), BF16), vm((NX, 8, 128), F32),
             vm((8, QR, W), F32), vm((4, QR, W), BF16), vm((4, QR, W), BF16), vm((4, QR, W), BF16), vm((4, QR, W), BF16),
             vm((8, QR, W), BF16), vm((8, QR, W), BF16), vm((PR, W), F32),
-            vm((NY, NC, QR, W), BF16), vm((8, 2, BR, 128), BF16),
+            vm((NY, NC, QR, W), BF16), vm((8, 2, BR, 128), BF16), vm((NY, NC, QR, FW), BF16), vm((8, 2, BR, 128), BF16),
             pltpu.SMEM((8,), jnp.int32), pltpu.SMEM((8, 7), jnp.int32), pltpu.SMEM((8,), jnp.int32),
             dma((5,)), dma((2, 14)), dma((2, 14)), dma((2, 12)), dma((2, 12)), dma((16,)), dma((16,)), dma((7,)), dma((7,)),
             dma((7,)), dma((7,)), dma((8, 3, 2)), dma((4, 3)), dma((2, 7)), dma((2, 7)), dma((4, 3)), dma((8, 2)),
             dma((3,)), dma((3,)), dma((2, 4, 4)), dma((2, 4, 4)), dma((8, 7)), dma((8, 7)), dma((2, 6)), dma((2, 6)), dma((4,)), dma((4,)),
-            dma((7, 2)), dma((7, 2)),
+            dma((7, 2)), dma((7, 2)), dma((2, 6)), dma((2, 6)), dma((4,)), dma((4,)), dma((7, 2)), dma((7, 2)),
         ],
         compiler_params=pltpu.CompilerParams(collective_id=0, has_side_effects=True, vmem_limit_bytes=60 * 2**20),
         cost_estimate=pl.CostEstimate(flops=10**10, bytes_accessed=4 * 10**6, transcendentals=10**6),

time: 125 us -> 125 us (level)
  no operation moved by 1% of the time
where the time goes in v2:
time: 125 us
  Pallas kernels  122 us (98%)
  local copies, waits for them, and re-layouts  2.33 us (2%)
    pallas_call x1, Pallas kernels, body(): pl.pallas_call(kernel, out_shape=(pltpu.VMEM((2, 128), F32), pltpu.VMEM((...  122 us

profile of v2, /device:TPU:1, one launch (start us, length us, event | category | flops | bytes accessed | tf_op | source)
XLA Modules:
  0.0 125.1 jit_solution(12430815893123748678)
XLA Ops:
  0.6 122.1 %shard_map.76 = (f32[2,128]{1,0:T(2,128)S(1)}, bf16[256,1024]{1,0:T(8,128)(2,1)S(1)}, bf16[512,1024]{1,0:T(8,128)(2,1)S(1)}) custom-call(s32[8]{0:T(128)} %pos_hbm.1, s32[8,7]{1,0:T(8,128)} %neg_hbm.1, s32[8]{0:T(128)} %cnt_hbm.1, bf16[256,1024]{1,0:T(8,128)(2,1)} %q_hbm.1, bf16[512,1024]{1,0:T(8,128)(2,1)} %p_hbm.1), custom_call_target="tpu_custom_call" | custom-call | flops 10000000000 | bytes 4000000 | tf_op jit(solution)/shard_map/pallas_call | solution.py:578
  122.8 0.6 copy.11
  123.3 0.8 copy.12
  124.1 1.0 copy.13
